TPU v7x, 32 devices: a whole 2x2x4 slice. The times are simulated.
32 devices in a mesh: group: 2 (over x), blk: 16 (over z, y, core).
Axes of the slice: x: 2, y: 2, z: 4, core: 2. Of those that a mesh axis runs over, the one named last changes fastest.
Arguments:
- features: bfloat16 [65536, 256], P(('group', 'blk')), parts along dimension 0, may hold values from -6 to 6
- cotangent: bfloat16 [65536, 256], P(('group', 'blk')), parts along dimension 0, may hold values from -6 to 6
- adjacency: bfloat16 [256, 8, 128, 128], P('blk'), may hold values from -0.25 to 0.25
- block_cols: int32 [256, 8], P('blk'), may hold values from 0 to 255, as said below
- block_count: int32 [256], P('blk'), may hold values from 2 to 8, as said below
- cluster_block: int32 [256], P('blk'), may hold values from 0 to 63, as said below
- cluster_slot: int32 [256, 128], P('blk'), may hold values from 0 to 127
- w_message: bfloat16 [256, 256], replicated, may hold values from -0.375 to 0.375
- w_upward: bfloat16 [256, 256], replicated, may hold values from -0.375 to 0.375
- w_self: bfloat16 [256, 256], replicated, may hold values from -0.375 to 0.375
- w_coarse: bfloat16 [256, 256], replicated, may hold values from -0.375 to 0.375
Outputs:
- layer_out: bfloat16 [65536, 256], P(('group', 'blk')), parts along dimension 0
- feature_grad: bfloat16 [65536, 256], P(('group', 'blk')), parts along dimension 0
- message_grad: float32 [512, 256], P('group'), parts along dimension 0
- upward_grad: float32 [512, 256], P('group'), parts along dimension 0
- self_grad: float32 [512, 256], P('group'), parts along dimension 0
- coarse_grad: float32 [512, 256], P('group'), parts along dimension 0
There are 2 independent parts, one for each index of `group`. A program takes and returns all parts, laid end to end along the dimension named above; an argument that names none is the same for every part. Nothing has to cross between parts.
Inputs may be any that keep to these rules, and one draw needn't show every extreme that they name: `block_cols`: slot 0 of row block r names r. Slot 1 of a row block among the first half of those held at index d of blk names a block from d * 16 minus half of 16 to d * 16 less one, and of one in the second half a block from (d + 1) * 16 to (d + 1) * 16 plus half of 16, less one, taken modulo 256. Every slot of a row block held at index d of blk names a block from d * 16 minus half of 16 to (d + 1) * 16 plus half of 16, less one, taken modulo 256. `block_count`: the counts of the 16 row blocks held at one index of blk sum to at most 80, and to exactly 80 at some index in every draw, where some row block has 8. `cluster_block`: A row block held at index d of blk names a coarse block from d * 4 minus half of 4 to (d + 1) * 4 plus half of 4, less one, taken modulo 64.
All inputs are finite; a program needn't handle non-finite values.
Results may differ from a plain program's by a relative error of at most 0.0075.
Values may be sent and summed in bfloat16 or wider, within the bound.
A program may use at most 128 MiB of HBM per device.

v0:
```python
import functools
import math

import jax
import jax.numpy as jnp
from jax import lax
from jax.experimental import pallas as pl
from jax.experimental.pallas import tpu as pltpu
from jax.sharding import PartitionSpec as P

MESH = pl.DeviceIdType.MESH
BF16 = jnp.bfloat16
F32 = jnp.float32


def mm(left, right):
    return lax.dot_general(left, right, (((1,), (0,)), ((), ())), preferred_element_type=F32)


def mm_nt(left, right):
    return lax.dot_general(left, right, (((1,), (1,)), ((), ())), preferred_element_type=F32)


def mm_tn(left, right):
    return lax.dot_general(left, right, (((0,), (0,)), ((), ())), preferred_element_type=F32)


def slope(value, sigma):
    return sigma * (1.0 + value * (1.0 - sigma))


def stages_of(count):
    stages, stride, rest = [], 1, count
    if rest % 2 == 0:
        stages.append((stride, 2))
        stride, rest = stride * 2, rest // 2
    while rest > 1:
        bits = rest.bit_length() - 1
        radix = 4 if rest % 4 == 0 and bits % 2 == 0 else 2
        stages.append((stride, radix))
        stride, rest = stride * radix, rest // radix
    return stages


def kernel(
    dims,
    meta,
    slot,
    w_m,
    w_u,
    w_s,
    w_c,
    feats,
    cots,
    adjs,
    layer_out,
    feature_grad,
    grad_m,
    grad_u,
    grad_s,
    grad_c,
    near,
    adj,
    adj_t,
    cot,
    total,
    msg,
    up,
    grad,
    back_m,
    hot_t,
    hot,
    chain,
    pool_chain,
    pool_send,
    pool_recv,
    pooled,
    coarse,
    c_slope,
    back_send,
    back_recv,
    back_pooled,
    row_send,
    row_recv,
    out_buf,
    acc,
    ring_send,
    ring_recv,
    gathered,
    local_sem,
    out_sem,
    ex_send,
    ex_recv,
    rs_send,
    rs_recv,
    ag_send,
    ag_recv,
):
    n, rb, slots, bs, cb = dims
    width = near.shape[2]
    half, edge, win = rb // 2, cb // 2, 2 * cb
    me = lax.axis_index("blk")
    left, right = lax.rem(me + n - 1, n), lax.rem(me + 1, n)
    stages = stages_of(n)
    o_prev = rb * slots
    o_last = 2 * rb * slots
    o_cidx = o_last + 2 * rb
    o_prevc = o_cidx + rb
    o_lastc = o_prevc + rb

    get_feats = pltpu.make_async_copy(feats, near.at[pl.ds(half, rb)], local_sem.at[0])
    get_cot = pltpu.make_async_copy(cots, cot, local_sem.at[1])
    get_adj = pltpu.make_async_copy(adjs, adj, local_sem.at[2])
    get_feats.start()
    get_adj.start()
    get_cot.start()

    barrier = pltpu.get_barrier_semaphore()
    friends = [left, right]
    for stride, radix in stages:
        digit = lax.rem(me // stride, radix)
        for off in range(1, radix):
            friends.append(me + (lax.rem(digit + off, radix) - digit) * stride)
    for friend in friends:
        pl.semaphore_signal(barrier, inc=1, device_id={"blk": friend}, device_id_type=MESH)
    near[2 * rb] = jnp.zeros((bs, width), BF16)
    pool_chain[rb] = jnp.zeros((bs, width), F32)
    chain[rb * slots] = jnp.zeros((bs, width), F32)
    get_feats.wait()
    pl.semaphore_wait(barrier, len(friends))

    def remote(src, dst, index, to):
        return pltpu.make_async_remote_copy(
            src_ref=src,
            dst_ref=dst,
            send_sem=ex_send.at[index],
            recv_sem=ex_recv.at[index],
            device_id={"blk": to},
            device_id_type=MESH,
        )

    halo = [
        remote(near.at[pl.ds(half, half)], near.at[pl.ds(rb + half, half)], 0, left),
        remote(near.at[pl.ds(rb, half)], near.at[pl.ds(0, half)], 1, right),
    ]
    for copy in halo:
        copy.start()

    def pool_body(r, carry):
        row = slot[pl.ds(r, 1), :]
        ids = lax.broadcasted_iota(jnp.int32, (bs, bs), 0)
        one = jnp.where(ids == row, 1.0, 0.0).astype(BF16)
        hot_t[r] = one
        pool_chain[r] = mm(one, near[half + r]) + pool_chain[meta[o_prevc + r]]
        return carry

    lax.fori_loop(0, rb, pool_body, 0, unroll=2)
    for w in range(win):
        pool_send[w] = pool_chain[meta[o_lastc + w]].astype(BF16)
    pool_ex = [
        remote(pool_send.at[pl.ds(0, cb)], pool_recv.at[pl.ds(cb, cb)], 2, left),
        remote(pool_send.at[pl.ds(cb, cb)], pool_recv.at[pl.ds(0, cb)], 3, right),
    ]
    for copy in pool_ex:
        copy.start()

    quad = 4

    def self_body(q, carry):
        x = near[pl.ds(half + q * quad, quad)].reshape(quad * bs, width)
        total[pl.ds(q * quad, quad)] = mm(x, w_s[...]).reshape(quad, bs, width)
        for k in range(quad):
            hot[q * quad + k] = hot_t[q * quad + k].T
        return carry

    lax.fori_loop(0, rb // quad, self_body, 0)
    get_adj.wait()

    def flip_body(r, carry):
        for e in range(slots):
            adj_t[r, pl.ds(e * bs, bs), :] = adj[r, e].T
        return carry

    lax.fori_loop(0, rb, flip_body, 0)

    for copy in pool_ex:
        copy.wait()
    for w in range(win):
        summed = pool_chain[meta[o_lastc + w]] + pool_recv[w].astype(F32)
        pooled[pl.ds(w * bs, bs), :] = (0.25 * summed).astype(BF16)
    pre = mm(pooled[...], w_c[...])
    sig = jax.nn.sigmoid(pre)
    coarse[...] = (pre * sig).astype(BF16).reshape(win, bs, width)
    c_slope[...] = slope(pre, sig)

    def up_body(q, carry):
        parts = []
        for k in range(quad):
            r = q * quad + k
            parts.append(mm(hot[r], coarse[meta[o_cidx + r]]).astype(BF16))
        block = jnp.concatenate(parts, axis=0)
        up[pl.ds(q * quad, quad)] = block.reshape(quad, bs, width)
        total[pl.ds(q * quad, quad)] += mm(block, w_u[...]).reshape(quad, bs, width)
        return carry

    lax.fori_loop(0, rb // quad, up_body, 0)
    get_cot.wait()
    for copy in halo:
        copy.wait()

    def fine_body(q, carry):
        parts = []
        for k in range(quad):
            r = q * quad + k
            lhs = jnp.concatenate([adj[r, e] for e in range(slots)], axis=1)
            rhs = jnp.concatenate([near[meta[r * slots + e]] for e in range(slots)], axis=0)
            parts.append(mm(lhs, rhs).astype(BF16))
        rows = pl.ds(q * quad, quad)
        flat = (quad * bs, width)
        message = jnp.concatenate(parts, axis=0)
        msg[rows] = message.reshape(quad, bs, width)
        pre = total[rows].reshape(flat) + mm(message, w_m[...])
        sig = jax.nn.sigmoid(pre)
        x = near[pl.ds(half + q * quad, quad)].reshape(flat).astype(F32)
        out_buf[rows] = (x + pre * sig).astype(BF16).reshape(quad, bs, width)
        c = cot[rows].reshape(flat).astype(F32)
        g = (c * slope(pre, sig)).astype(BF16)
        grad[rows] = g.reshape(quad, bs, width)
        back_m[rows] = mm_nt(g, w_m[...]).astype(BF16).reshape(quad, bs, width)
        total[rows] = (c + mm_nt(g, w_s[...])).reshape(quad, bs, width)
        back_u = mm_nt(g, w_u[...]).astype(BF16)
        for k in range(quad):
            r = q * quad + k
            part = mm(hot_t[r], back_u[k * bs : (k + 1) * bs])
            pool_chain[r] = part + pool_chain[meta[o_prevc + r]]
        return carry

    lax.fori_loop(0, rb // quad, fine_body, 0)
    put_out = pltpu.make_async_copy(out_buf, layer_out, out_sem.at[0])
    put_out.start()
    for w in range(win):
        back_send[w] = pool_chain[meta[o_lastc + w]].astype(BF16)
    back_ex = [
        remote(back_send.at[pl.ds(0, cb)], back_recv.at[pl.ds(cb, cb)], 4, left),
        remote(back_send.at[pl.ds(cb, cb)], back_recv.at[pl.ds(0, cb)], 5, right),
    ]
    for copy in back_ex:
        copy.start()

    scale = 1.0 / math.sqrt(n * rb * bs)
    acc[...] = jnp.zeros_like(acc)

    def grads_body(q, carry):
        rows = pl.ds(q * quad, quad)
        flat = (quad * bs, width)
        g = grad[rows].reshape(flat)
        x = near[pl.ds(half + q * quad, quad)].reshape(flat)
        acc[pl.ds(0, width)] += mm_tn(msg[rows].reshape(flat), g)
        acc[pl.ds(width, width)] += mm_tn(up[rows].reshape(flat), g)
        acc[pl.ds(2 * width, width)] += mm_tn(x, g)
        return carry

    lax.fori_loop(0, rb // quad, grads_body, 0)

    def coarse_body(w, carry):
        rows = pl.ds(pl.multiple_of(w * bs, bs), bs)
        part = (pool_chain[meta[o_lastc + w]] * c_slope[rows, :]).astype(BF16)
        acc[pl.ds(3 * width, width)] += mm_tn(pooled[rows, :], part)
        return carry

    lax.fori_loop(0, win, coarse_body, 0)
    acc[...] = acc[...] * scale

    height = acc.shape[0]
    plan = []
    base, seg, index, slot_row = 0, height, 0, 0
    for stride, radix in stages:
        digit = lax.rem(me // stride, radix)
        sub = seg // radix
        plan.append((stride, radix, digit, base, seg, sub, index, slot_row))
        base = base + digit * sub
        seg = sub
        slot_row += (radix - 1) * sub
        index += radix - 1

    def rows_at(start, count):
        return pl.ds(pl.multiple_of(start, 16), count)

    def scatter_start(k):
        stride, radix, digit, base, seg, sub, index, slot_row = plan[k]
        ring_send[k, rows_at(base, seg), :] = acc[rows_at(base, seg), :].astype(BF16)
        copies = []
        for off in range(1, radix):
            other = lax.rem(digit + off, radix)
            copies.append(
                pltpu.make_async_remote_copy(
                    src_ref=ring_send.at[k, rows_at(base + other * sub, sub), :],
                    dst_ref=ring_recv.at[pl.ds(slot_row + (off - 1) * sub, sub), :],
                    send_sem=rs_send.at[index + off - 1],
                    recv_sem=rs_recv.at[index + off - 1],
                    device_id={"blk": me + (other - digit) * stride},
                    device_id_type=MESH,
                )
            )
        for copy in copies:
            copy.start()
        return copies

    def scatter_end(k, copies):
        stride, radix, digit, base, seg, sub, index, slot_row = plan[k]
        for copy in copies:
            copy.wait()
        mine = rows_at(base + digit * sub, sub)
        value = acc[mine, :]
        for off in range(1, radix):
            value = value + ring_recv[pl.ds(slot_row + (off - 1) * sub, sub), :].astype(F32)
        acc[mine, :] = value

    def gather_start(k):
        stride, radix, digit, base, seg, sub, index, slot_row = plan[k]
        mine = rows_at(base + digit * sub, sub)
        copies = []
        for off in range(1, radix):
            other = lax.rem(digit + off, radix)
            copies.append(
                pltpu.make_async_remote_copy(
                    src_ref=gathered.at[mine, :],
                    dst_ref=gathered.at[mine, :],
                    send_sem=ag_send.at[index + off - 1],
                    recv_sem=ag_recv.at[index + off - 1],
                    device_id={"blk": me + (other - digit) * stride},
                    device_id_type=MESH,
                )
            )
        for copy in copies:
            copy.start()
        return copies

    flying = scatter_start(0)

    def flow_body(r, carry):
        prod = mm(adj_t[r], back_m[r])
        for e in range(slots):
            s = r * slots + e
            chain[s] = prod[e * bs : (e + 1) * bs] + chain[meta[o_prev + s]]
        return carry

    lax.fori_loop(0, rb, flow_body, 0)
    for b in range(half):
        row_send[b] = chain[meta[o_last + b]].astype(BF16)
        row_send[half + b] = chain[meta[o_last + half + rb + b]].astype(BF16)
    row_ex = [
        remote(row_send.at[pl.ds(0, half)], row_recv.at[pl.ds(half, half)], 6, left),
        remote(row_send.at[pl.ds(half, half)], row_recv.at[pl.ds(0, half)], 7, right),
    ]
    for copy in row_ex:
        copy.start()

    scatter_end(0, flying)
    if len(stages) > 1:
        flying = scatter_start(1)

    for copy in back_ex:
        copy.wait()
    for w in range(win):
        rows = pl.ds(w * bs, bs)
        summed = pool_chain[meta[o_lastc + w]] + back_recv[w].astype(F32)
        g = (summed * c_slope[rows, :]).astype(BF16)
        back_pooled[w] = mm_nt(g, w_c[...]).astype(BF16)

    def spread_body(r, carry):
        spread = mm(hot[r], back_pooled[meta[o_cidx + r]])
        total[r] += 0.25 * spread + chain[meta[o_last + half + r]]
        return carry

    lax.fori_loop(0, rb, spread_body, 0, unroll=2)

    done = 1
    if len(stages) > 1:
        scatter_end(1, flying)
        done = 2
    if len(stages) > 2:
        flying = scatter_start(2)

    put_out.wait()
    for copy in row_ex:
        copy.wait()

    def last_body(r, carry):
        out_buf[r] = (total[r] + row_recv[r].astype(F32)).astype(BF16)
        return carry

    lax.fori_loop(0, rb, last_body, 0, unroll=2)
    put_grad = pltpu.make_async_copy(out_buf, feature_grad, out_sem.at[1])
    put_grad.start()

    if len(stages) > 2:
        scatter_end(2, flying)
        done = 3
    for k in range(done, len(stages)):
        scatter_end(k, scatter_start(k))
    stride, radix, digit, base, seg, sub, index, slot_row = plan[-1]
    mine = rows_at(base + digit * sub, sub)
    gathered[mine, :] = acc[mine, :].astype(BF16)
    for k in reversed(range(len(stages))):
        for copy in gather_start(k):
            copy.wait()
    for k, out in enumerate((grad_m, grad_u, grad_s, grad_c)):
        out[...] = gathered[pl.ds(k * width, width), :].astype(F32)
    put_grad.wait()


def on_device(
    features,
    cotangent,
    adjacency,
    block_cols,
    block_count,
    cluster_block,
    cluster_slot,
    w_message,
    w_upward,
    w_self,
    w_coarse,
):
    rb, slots = block_cols.shape
    bs = adjacency.shape[2]
    width = features.shape[1]
    n = lax.axis_size("blk")
    position = lax.axis_index("blk")
    cb = rb // 4
    half, edge, win = rb // 2, cb // 2, 2 * cb
    count = rb * slots

    live = jnp.arange(slots, dtype=jnp.int32)[None, :] < block_count[:, None]
    cols = jnp.clip(jnp.remainder(block_cols - (position * rb - half), n * rb), 0, 2 * rb - 1)
    cols = jnp.where(live, cols, 2 * rb).reshape(count)
    alive = live.reshape(count)
    ids = jnp.arange(count, dtype=jnp.int32)
    same = (cols[:, None] == cols[None, :]) & alive[None, :] & (ids[None, :] < ids[:, None])
    prev = jnp.max(jnp.where(same, ids[None, :], -1), axis=1)
    prev = jnp.where(prev < 0, count, prev)
    wins = jnp.arange(2 * rb, dtype=jnp.int32)
    last = jnp.max(jnp.where(cols[None, :] == wins[:, None], ids[None, :], -1), axis=1)
    last = jnp.where(last < 0, count, last)
    cidx = jnp.clip(jnp.remainder(cluster_block - (position * cb - edge), n * cb), 0, win - 1)
    rids = jnp.arange(rb, dtype=jnp.int32)
    samec = (cidx[:, None] == cidx[None, :]) & (rids[None, :] < rids[:, None])
    prevc = jnp.max(jnp.where(samec, rids[None, :], -1), axis=1)
    prevc = jnp.where(prevc < 0, rb, prevc)
    cwins = jnp.arange(win, dtype=jnp.int32)
    lastc = jnp.max(jnp.where(cidx[None, :] == cwins[:, None], rids[None, :], -1), axis=1)
    lastc = jnp.where(lastc < 0, rb, lastc)
    meta = jnp.concatenate([cols, prev, last, cidx, prevc, lastc])

    stages = stages_of(n)
    links = max(sum(radix - 1 for _, radix in stages), 1)
    height = 4 * width
    rows, seg = 0, height
    for _, radix in stages:
        seg //= radix
        rows += (radix - 1) * seg
    vmem = pl.BlockSpec(memory_space=pltpu.VMEM)
    hbm = pl.BlockSpec(memory_space=pl.ANY)
    blocks = (rb, bs, width)
    outs = pl.pallas_call(
        functools.partial(kernel, (n, rb, slots, bs, cb)),
        out_shape=[
            jax.ShapeDtypeStruct(blocks, BF16),
            jax.ShapeDtypeStruct(blocks, BF16),
        ]
        + [jax.ShapeDtypeStruct((width, width), F32)] * 4,
        in_specs=[pl.BlockSpec(memory_space=pltpu.SMEM)] + [vmem] * 5 + [hbm] * 3,
        out_specs=[hbm, hbm] + [vmem] * 4,
        scratch_shapes=[
            pltpu.VMEM((2 * rb + 1, bs, width), BF16),
            pltpu.VMEM((rb, slots, bs, bs), BF16),
            pltpu.VMEM((rb, slots * bs, bs), BF16),
            pltpu.VMEM(blocks, BF16),
            pltpu.VMEM(blocks, F32),
            pltpu.VMEM(blocks, BF16),
            pltpu.VMEM(blocks, BF16),
            pltpu.VMEM(blocks, BF16),
            pltpu.VMEM(blocks, BF16),
            pltpu.VMEM((rb, bs, bs), BF16),
            pltpu.VMEM((rb, bs, bs), BF16),
            pltpu.VMEM((count + 1, bs, width), F32),
            pltpu.VMEM((rb + 1, bs, width), F32),
            pltpu.VMEM((win, bs, width), BF16),
            pltpu.VMEM((win, bs, width), BF16),
            pltpu.VMEM((win * bs, width), BF16),
            pltpu.VMEM((win, bs, width), BF16),
            pltpu.VMEM((win * bs, width), F32),
            pltpu.VMEM((win, bs, width), BF16),
            pltpu.VMEM((win, bs, width), BF16),
            pltpu.VMEM((win, bs, width), BF16),
            pltpu.VMEM(blocks, BF16),
            pltpu.VMEM(blocks, BF16),
            pltpu.VMEM(blocks, BF16),
            pltpu.VMEM((height, width), F32),
            pltpu.VMEM((max(len(stages), 1), height, width), BF16),
            pltpu.VMEM((max(rows, 16), width), BF16),
            pltpu.VMEM((height, width), BF16),
            pltpu.SemaphoreType.DMA((3,)),
            pltpu.SemaphoreType.DMA((2,)),
            pltpu.SemaphoreType.DMA((8,)),
            pltpu.SemaphoreType.DMA((8,)),
            pltpu.SemaphoreType.DMA((links,)),
            pltpu.SemaphoreType.DMA((links,)),
            pltpu.SemaphoreType.DMA((links,)),
            pltpu.SemaphoreType.DMA((links,)),
        ],
        compiler_params=pltpu.CompilerParams(
            collective_id=0, has_side_effects=True, vmem_limit_bytes=56 * 1024 * 1024
        ),
    )(
        meta,
        cluster_slot,
        w_message,
        w_upward,
        w_self,
        w_coarse,
        features.reshape(blocks),
        cotangent.reshape(blocks),
        adjacency,
    )
    return (outs[0].reshape(features.shape), outs[1].reshape(features.shape), *outs[2:])


def solution(mesh):
    in_specs = (
        P(("group", "blk"), None),
        P(("group", "blk"), None),
        P("blk", None, None, None),
        P("blk", None),
        P("blk"),
        P("blk"),
        P("blk", None),
        P(),
        P(),
        P(),
        P(),
    )
    out_specs = (
        P(("group", "blk"), None),
        P(("group", "blk"), None),
        P("group", None),
        P("group", None),
        P("group", None),
        P("group", None),
    )
    return jax.shard_map(
        on_device, mesh=mesh, in_specs=in_specs, out_specs=out_specs, check_vma=False
    )
```

profile of v0, /device:TPU:0, one launch (start us, length us, event | category | flops | bytes accessed | tf_op | source)
XLA Modules:
  0.0 78.3 jit_solution(11151303952069387627)
XLA Ops:
  0.6 0.7 fusion.5
  1.3 0.1 select_reduce_fusion.3
  1.4 0.2 select_reduce_fusion.2
  1.6 0.7 iota_compare_fusion.4
  2.3 0.1 copy.22
  2.4 0.1 lt.84
  2.5 0.7 fusion.4
  3.2 0.1 copy.21
  3.3 0.1 reshape.46
  3.3 0.2 select_reduce_fusion
  3.5 0.1 select_reduce_fusion.1
  3.7 0.7 concatenate.3.meta
  4.3 66.4 %shard_map.154 = (bf16[16,128,256]{2,1,0:T(8,128)(2,1)}, bf16[16,128,256]{2,1,0:T(8,128)(2,1)}, f32[256,256]{1,0:T(8,128)}, f32[256,256]{1,0:T(8,128)}, f32[256,256]{1,0:T(8,128)}, /*index=5*/f32[256,256]{1,0:T(8,128)}) custom-call(s32[328]{0:T(512)} %concatenate.3.meta, s32[16,128]{1,0:T(8,128)} %slot.1, bf16[256,256]{1,0:T(8,128)(2,1)} %w_m.1, ...), custom_call_target="tpu_custom_call" | custom-call | tf_op jit(solution)/shard_map/pallas_call | solution.py:466
  70.8 0.0 copy-start.3
  70.8 0.0 copy-start.2
  70.8 0.0 copy-start.1
  70.8 0.0 copy-start
  70.8 2.3 %copy.29 = bf16[2048,256]{1,0:T(8,128)(2,1)} copy(bf16[2048,256]{1,0:T(8,128)(2,1)} %bitcast.7) | data formatting | bytes 2097152
  73.2 2.3 %copy.30 = bf16[2048,256]{1,0:T(8,128)(2,1)} copy(bf16[2048,256]{1,0:T(8,128)(2,1)} %bitcast.6) | data formatting | bytes 2097152
  75.4 0.0 copy-done.3
  75.4 0.7 copy.31
  76.1 0.0 copy-done.2
  76.1 0.7 copy.32
  76.8 0.0 copy-done.1
  76.9 0.7 copy.33
  77.6 0.0 copy-done
  77.6 0.7 copy.34
  (4 shorter events, 0.0 us)
Async XLA Ops:
  70.8 4.6 %copy-start.3 = (f32[256,256]{1,0:T(8,128)S(1)}, f32[256,256]{1,0:T(8,128)}, u32[]{:S(2)}) copy-start(f32[256,256]{1,0:T(8,128)} %get-tuple-element.26) | copy-start | bytes 786436
  70.8 5.3 %copy-start.2 = (f32[256,256]{1,0:T(8,128)S(1)}, f32[256,256]{1,0:T(8,128)}, u32[]{:S(2)}) copy-start(f32[256,256]{1,0:T(8,128)} %get-tuple-element.27) | copy-start | bytes 786436
  70.8 6.0 %copy-start.1 = (f32[256,256]{1,0:T(8,128)S(1)}, f32[256,256]{1,0:T(8,128)}, u32[]{:S(2)}) copy-start(f32[256,256]{1,0:T(8,128)} %get-tuple-element.28) | copy-start | bytes 786436
  70.8 6.7 %copy-start = (f32[256,256]{1,0:T(8,128)S(1)}, f32[256,256]{1,0:T(8,128)}, u32[]{:S(2)}) copy-start(f32[256,256]{1,0:T(8,128)} %get-tuple-element.29) | copy-start | bytes 786436
where the time goes:
time: 78.5 us; the launch traced here: 78.3 us
  Pallas kernels  66.4 us (85%)
  local copies, waits for them, and re-layouts  8.44 us (11%)
  other arithmetic  2.67 us (3%)
    pallas_call x1, Pallas kernels, on_device(): pl.pallas_call(functools.partial(kernel, (n, rb, slots, bs, cb)), out_sha...  66.4 us
    unnamed x14, local copies, waits for them, and re-layouts  7.43 us

commit v1 on v0

--- a/solution.py
+++ b/solution.py
@@ -39,7 +39,72 @@
         radix = 4 if rest % 4 == 0 and bits % 2 == 0 else 2
         stages.append((stride, radix))
         stride, rest = stride * radix, rest // radix
-    return stages
+    return stages[:1] + stages[1:][::-1]
+
+
+def order_kernel(dims, cols_in, counts, clusters, meta):
+    n, rb, slots, cb = dims
+    half, edge, win = rb // 2, cb // 2, 2 * cb
+    me = lax.axis_index("blk")
+    count = rb * slots
+    o_prev = count
+    o_last = 2 * count
+    o_cidx = o_last + 2 * rb
+    o_prevc = o_cidx + rb
+    o_lastc = o_prevc + rb
+
+    def fill(start, size, value):
+        def body(i, carry):
+            meta[start + i] = value
+            return carry
+
+        lax.fori_loop(0, size, body, 0, unroll=8)
+
+    fill(o_last, 2 * rb, count)
+    fill(o_lastc, win, rb)
+
+    def row(r, carry):
+        live = counts[r]
+        for e in range(slots):
+            s = r * slots + e
+            there = cols_in[r, e] - (me * rb - half)
+            there = jnp.where(there < 0, there + n * rb, there)
+            there = jnp.where(there >= n * rb, there - n * rb, there)
+            there = jnp.minimum(jnp.maximum(there, 0), 2 * rb - 1)
+            on = e < live
+            before = meta[o_last + there]
+            meta[s] = jnp.where(on, there, 2 * rb)
+            meta[o_prev + s] = jnp.where(on, before, count)
+            meta[o_last + there] = jnp.where(on, s, before)
+        c = clusters[r] - (me * cb - edge)
+        c = jnp.where(c < 0, c + n * cb, c)
+        c = jnp.where(c >= n * cb, c - n * cb, c)
+        c = jnp.minimum(jnp.maximum(c, 0), win - 1)
+        meta[o_cidx + r] = c
+        meta[o_prevc + r] = meta[o_lastc + c]
+        meta[o_lastc + c] = r
+        return carry
+
+    lax.fori_loop(0, rb, row, 0)
+
+
+def finish_kernel(pieces, a, b, g, a_out, b_out, m_out, u_out, s_out, c_out, buf, sem):
+    copies = []
+    step = a.shape[0] // pieces
+    for k in range(pieces):
+        rows = pl.ds(k * step, step)
+        copies.append(pltpu.make_async_copy(a.at[rows], a_out.at[rows], sem.at[2 * k]))
+        copies.append(pltpu.make_async_copy(b.at[rows], b_out.at[rows], sem.at[2 * k + 1]))
+    load = pltpu.make_async_copy(g, buf, sem.at[2 * pieces])
+    load.start()
+    for copy in copies:
+        copy.start()
+    load.wait()
+    width = m_out.shape[0]
+    for k, out in enumerate((m_out, u_out, s_out, c_out)):
+        out[...] = buf[pl.ds(k * width, width), :].astype(F32)
+    for copy in copies:
+        copy.wait()
 
 
 def kernel(
@@ -55,10 +120,7 @@
     adjs,
     layer_out,
     feature_grad,
-    grad_m,
-    grad_u,
-    grad_s,
-    grad_c,
+    gathered,
     near,
     adj,
     adj_t,
@@ -86,7 +148,6 @@
     acc,
     ring_send,
     ring_recv,
-    gathered,
     local_sem,
     out_sem,
     ex_send,
@@ -345,7 +406,11 @@
             chain[s] = prod[e * bs : (e + 1) * bs] + chain[meta[o_prev + s]]
         return carry
 
-    lax.fori_loop(0, rb, flow_body, 0)
+    lax.fori_loop(0, rb // 2, flow_body, 0)
+    scatter_end(0, flying)
+    if len(stages) > 1:
+        flying = scatter_start(1)
+    lax.fori_loop(rb // 2, rb, flow_body, 0)
     for b in range(half):
         row_send[b] = chain[meta[o_last + b]].astype(BF16)
         row_send[half + b] = chain[meta[o_last + half + rb + b]].astype(BF16)
@@ -355,10 +420,10 @@
     ]
     for copy in row_ex:
         copy.start()
-
-    scatter_end(0, flying)
     if len(stages) > 1:
-        flying = scatter_start(1)
+        scatter_end(1, flying)
+    if len(stages) > 2:
+        flying = scatter_start(2)
 
     for copy in back_ex:
         copy.wait()
@@ -375,38 +440,33 @@
 
     lax.fori_loop(0, rb, spread_body, 0, unroll=2)
 
-    done = 1
-    if len(stages) > 1:
-        scatter_end(1, flying)
-        done = 2
-    if len(stages) > 2:
-        flying = scatter_start(2)
-
-    put_out.wait()
-    for copy in row_ex:
-        copy.wait()
-
-    def last_body(r, carry):
-        out_buf[r] = (total[r] + row_recv[r].astype(F32)).astype(BF16)
-        return carry
-
-    lax.fori_loop(0, rb, last_body, 0, unroll=2)
-    put_grad = pltpu.make_async_copy(out_buf, feature_grad, out_sem.at[1])
-    put_grad.start()
-
     if len(stages) > 2:
         scatter_end(2, flying)
-        done = 3
-    for k in range(done, len(stages)):
+    for k in range(3, len(stages)):
         scatter_end(k, scatter_start(k))
     stride, radix, digit, base, seg, sub, index, slot_row = plan[-1]
     mine = rows_at(base + digit * sub, sub)
     gathered[mine, :] = acc[mine, :].astype(BF16)
-    for k in reversed(range(len(stages))):
+    for k in reversed(range(2, len(stages))):
         for copy in gather_start(k):
             copy.wait()
-    for k, out in enumerate((grad_m, grad_u, grad_s, grad_c)):
-        out[...] = gathered[pl.ds(k * width, width), :].astype(F32)
+    flying = gather_start(1) if len(stages) > 1 else []
+
+    put_out.wait()
+    for copy in row_ex:
+        copy.wait()
+
+    def last_body(r, carry):
+        out_buf[r] = (total[r] + row_recv[r].astype(F32)).astype(BF16)
+        return carry
+
+    lax.fori_loop(0, rb, last_body, 0, unroll=2)
+    put_grad = pltpu.make_async_copy(out_buf, feature_grad, out_sem.at[1])
+    put_grad.start()
+    for copy in flying:
+        copy.wait()
+    for copy in gather_start(0):
+        copy.wait()
     put_grad.wait()
 
 
@@ -427,31 +487,17 @@
     bs = adjacency.shape[2]
     width = features.shape[1]
     n = lax.axis_size("blk")
-    position = lax.axis_index("blk")
     cb = rb // 4
-    half, edge, win = rb // 2, cb // 2, 2 * cb
+    win = 2 * cb
     count = rb * slots
 
-    live = jnp.arange(slots, dtype=jnp.int32)[None, :] < block_count[:, None]
-    cols = jnp.clip(jnp.remainder(block_cols - (position * rb - half), n * rb), 0, 2 * rb - 1)
-    cols = jnp.where(live, cols, 2 * rb).reshape(count)
-    alive = live.reshape(count)
-    ids = jnp.arange(count, dtype=jnp.int32)
-    same = (cols[:, None] == cols[None, :]) & alive[None, :] & (ids[None, :] < ids[:, None])
-    prev = jnp.max(jnp.where(same, ids[None, :], -1), axis=1)
-    prev = jnp.where(prev < 0, count, prev)
-    wins = jnp.arange(2 * rb, dtype=jnp.int32)
-    last = jnp.max(jnp.where(cols[None, :] == wins[:, None], ids[None, :], -1), axis=1)
-    last = jnp.where(last < 0, count, last)
-    cidx = jnp.clip(jnp.remainder(cluster_block - (position * cb - edge), n * cb), 0, win - 1)
-    rids = jnp.arange(rb, dtype=jnp.int32)
-    samec = (cidx[:, None] == cidx[None, :]) & (rids[None, :] < rids[:, None])
-    prevc = jnp.max(jnp.where(samec, rids[None, :], -1), axis=1)
-    prevc = jnp.where(prevc < 0, rb, prevc)
-    cwins = jnp.arange(win, dtype=jnp.int32)
-    lastc = jnp.max(jnp.where(cidx[None, :] == cwins[:, None], rids[None, :], -1), axis=1)
-    lastc = jnp.where(lastc < 0, rb, lastc)
-    meta = jnp.concatenate([cols, prev, last, cidx, prevc, lastc])
+    smem = pl.BlockSpec(memory_space=pltpu.SMEM)
+    meta = pl.pallas_call(
+        functools.partial(order_kernel, (n, rb, slots, cb)),
+        out_shape=jax.ShapeDtypeStruct((2 * count + 4 * rb + win,), jnp.int32),
+        in_specs=[smem] * 3,
+        out_specs=smem,
+    )(block_cols, block_count, cluster_block)
 
     stages = stages_of(n)
     links = max(sum(radix - 1 for _, radix in stages), 1)
@@ -469,9 +515,9 @@
             jax.ShapeDtypeStruct(blocks, BF16),
             jax.ShapeDtypeStruct(blocks, BF16),
         ]
-        + [jax.ShapeDtypeStruct((width, width), F32)] * 4,
-        in_specs=[pl.BlockSpec(memory_space=pltpu.SMEM)] + [vmem] * 5 + [hbm] * 3,
-        out_specs=[hbm, hbm] + [vmem] * 4,
+        + [jax.ShapeDtypeStruct((height, width), BF16)],
+        in_specs=[smem] + [vmem] * 5 + [hbm] * 3,
+        out_specs=[hbm, hbm, vmem],
         scratch_shapes=[
             pltpu.VMEM((2 * rb + 1, bs, width), BF16),
             pltpu.VMEM((rb, slots, bs, bs), BF16),
@@ -500,7 +546,6 @@
             pltpu.VMEM((height, width), F32),
             pltpu.VMEM((max(len(stages), 1), height, width), BF16),
             pltpu.VMEM((max(rows, 16), width), BF16),
-            pltpu.VMEM((height, width), BF16),
             pltpu.SemaphoreType.DMA((3,)),
             pltpu.SemaphoreType.DMA((2,)),
             pltpu.SemaphoreType.DMA((8,)),
@@ -524,6 +569,21 @@
         cotangent.reshape(blocks),
         adjacency,
     )
+    pieces = 4 if rb % 4 == 0 else 1
+    outs = pl.pallas_call(
+        functools.partial(finish_kernel, pieces),
+        out_shape=[
+            jax.ShapeDtypeStruct(blocks, BF16),
+            jax.ShapeDtypeStruct(blocks, BF16),
+        ]
+        + [jax.ShapeDtypeStruct((width, width), F32)] * 4,
+        in_specs=[hbm] * 3,
+        out_specs=[hbm, hbm] + [vmem] * 4,
+        scratch_shapes=[
+            pltpu.VMEM((height, width), BF16),
+            pltpu.SemaphoreType.DMA((2 * pieces + 1,)),
+        ],
+    )(*outs)
     return (outs[0].reshape(features.shape), outs[1].reshape(features.shape), *outs[2:])
 
 

time: 78.5 us -> 136 us (1.73)
  Pallas kernels: 66.4 us -> 134 us
  local copies, waits for them, and re-layouts: 8.44 us -> 1.36 us
  other arithmetic: 2.67 us -> 0 us
    pallas_call x0 -> x2, Pallas kernels: none -> 68.3 us  [the longest x1 65.7 us: on_device(): pl.pallas_call(functools.partial(finish_kernel, pieces), out_shape=[jax.S...]
    unnamed x14 -> x1, local copies, waits for them, and re-layouts: 7.43 us -> 1.36 us
where the time goes in v1:
time: 136 us
  Pallas kernels  134 us (99%)
  local copies, waits for them, and re-layouts  1.36 us (1%)
    pallas_call x1, Pallas kernels, on_device(): pl.pallas_call(functools.partial(finish_kernel, pieces), out_shape=[jax.S...  65.7 us
    pallas_call x1, Pallas kernels, on_device(): pl.pallas_call(functools.partial(kernel, (n, rb, slots, bs, cb)), out_sha...  65.3 us

profile of v1, /device:TPU:0, one launch (start us, length us, event | category | flops | bytes accessed | tf_op | source)
XLA Modules:
  0.0 135.6 jit_solution(14361733657248775282)
XLA Ops:
  0.6 1.4 copy.17.cols_in
  2.0 2.6 %shard_map.154.meta = s32[328]{0:T(512)} custom-call(s32[16,8]{1,0:T(8,128)} %copy.17.cols_in, s32[16]{0:T(128)} %counts.1, s32[16]{0:T(128)} %clusters.1), custom_call_target="tpu_custom_call" | custom-call | tf_op jit(solution)/shard_map/pallas_call | solution.py:495
  4.6 65.3 %shard_map.155 = (bf16[16,128,256]{2,1,0:T(8,128)(2,1)}, bf16[16,128,256]{2,1,0:T(8,128)(2,1)}, bf16[1024,256]{1,0:T(8,128)(2,1)}) custom-call(s32[328]{0:T(512)} %shard_map.154.meta, s32[16,128]{1,0:T(8,128)} %slot.1, bf16[256,256]{1,0:T(8,128)(2,1)} %w_m.1, bf16[256,256]{1,0:T(8,128)(2,1)} %w_u.1, bf16[256,256]{1,0:T(8,128)(2,1)} %w_s.1, ...), custom_call_target="tpu_custom_call" | custom-call | tf_op jit(solution)/shard_map/pallas_call | solution.py:512
  69.9 65.7 %shard_map.156 = (bf16[16,128,256]{2,1,0:T(8,128)(2,1)}, bf16[16,128,256]{2,1,0:T(8,128)(2,1)}, f32[256,256]{1,0:T(8,128)}, f32[256,256]{1,0:T(8,128)}, f32[256,256]{1,0:T(8,128)}, /*index=5*/f32[256,256]{1,0:T(8,128)}) custom-call(bf16[16,128,256]{2,1,0:T(8,128)(2,1)} %get-tuple-element.15.a, bf16[16,128,256]{2,1,0:T(8,128)(2,1)} %get-tuple-element.16.b, ...), custom_call_target="tpu_custom_call" | custom-call | tf_op jit(solution)/shard_map/pallas_call | solution.py:573

commit v2 on v1

--- a/solution.py
+++ b/solution.py
@@ -67,7 +67,7 @@
         live = counts[r]
         for e in range(slots):
             s = r * slots + e
-            there = cols_in[r, e] - (me * rb - half)
+            there = cols_in[s] - (me * rb - half)
             there = jnp.where(there < 0, there + n * rb, there)
             there = jnp.where(there >= n * rb, there - n * rb, there)
             there = jnp.minimum(jnp.maximum(there, 0), 2 * rb - 1)
@@ -88,23 +88,27 @@
     lax.fori_loop(0, rb, row, 0)
 
 
-def finish_kernel(pieces, a, b, g, a_out, b_out, m_out, u_out, s_out, c_out, buf, sem):
-    copies = []
+def finish_kernel(pieces, a, b, g, a_out, b_out, m_out, u_out, s_out, c_out, a_buf, b_buf, buf, sem):
+    loads, stores = [], []
     step = a.shape[0] // pieces
+    load = pltpu.make_async_copy(g, buf, sem.at[0, 2 * pieces])
+    load.start()
     for k in range(pieces):
         rows = pl.ds(k * step, step)
-        copies.append(pltpu.make_async_copy(a.at[rows], a_out.at[rows], sem.at[2 * k]))
-        copies.append(pltpu.make_async_copy(b.at[rows], b_out.at[rows], sem.at[2 * k + 1]))
-    load = pltpu.make_async_copy(g, buf, sem.at[2 * pieces])
-    load.start()
-    for copy in copies:
-        copy.start()
+        for j, (src, mid, dst) in enumerate(((a, a_buf, a_out), (b, b_buf, b_out))):
+            at = 2 * k + j
+            loads.append(pltpu.make_async_copy(src.at[rows], mid.at[rows], sem.at[0, at]))
+            stores.append(pltpu.make_async_copy(mid.at[rows], dst.at[rows], sem.at[1, at]))
+            loads[-1].start()
     load.wait()
     width = m_out.shape[0]
     for k, out in enumerate((m_out, u_out, s_out, c_out)):
         out[...] = buf[pl.ds(k * width, width), :].astype(F32)
-    for copy in copies:
-        copy.wait()
+    for come, go in zip(loads, stores):
+        come.wait()
+        go.start()
+    for go in stores:
+        go.wait()
 
 
 def kernel(
@@ -200,11 +204,14 @@
             device_id_type=MESH,
         )
 
-    halo = [
-        remote(near.at[pl.ds(half, half)], near.at[pl.ds(rb + half, half)], 0, left),
-        remote(near.at[pl.ds(rb, half)], near.at[pl.ds(0, half)], 1, right),
-    ]
-    for copy in halo:
+    lead = max(half // 4, 1)
+    halo = []
+    for k, (start, size) in enumerate(((0, lead), (lead, half - lead))):
+        for j, (here, there, to) in enumerate(((half, rb + half, left), (rb, 0, right))):
+            src = near.at[pl.ds(here + start, size)]
+            dst = near.at[pl.ds(there + start, size)]
+            halo.append(remote(src, dst, 2 * k + j, to))
+    for copy in halo[:2]:
         copy.start()
 
     def pool_body(r, carry):
@@ -219,10 +226,12 @@
     for w in range(win):
         pool_send[w] = pool_chain[meta[o_lastc + w]].astype(BF16)
     pool_ex = [
-        remote(pool_send.at[pl.ds(0, cb)], pool_recv.at[pl.ds(cb, cb)], 2, left),
-        remote(pool_send.at[pl.ds(cb, cb)], pool_recv.at[pl.ds(0, cb)], 3, right),
+        remote(pool_send.at[pl.ds(0, cb)], pool_recv.at[pl.ds(cb, cb)], 4, left),
+        remote(pool_send.at[pl.ds(cb, cb)], pool_recv.at[pl.ds(0, cb)], 5, right),
     ]
     for copy in pool_ex:
+        copy.start()
+    for copy in halo[2:]:
         copy.start()
 
     quad = 4
@@ -302,8 +311,8 @@
     for w in range(win):
         back_send[w] = pool_chain[meta[o_lastc + w]].astype(BF16)
     back_ex = [
-        remote(back_send.at[pl.ds(0, cb)], back_recv.at[pl.ds(cb, cb)], 4, left),
-        remote(back_send.at[pl.ds(cb, cb)], back_recv.at[pl.ds(0, cb)], 5, right),
+        remote(back_send.at[pl.ds(0, cb)], back_recv.at[pl.ds(cb, cb)], 6, left),
+        remote(back_send.at[pl.ds(cb, cb)], back_recv.at[pl.ds(0, cb)], 7, right),
     ]
     for copy in back_ex:
         copy.start()
@@ -414,16 +423,24 @@
     for b in range(half):
         row_send[b] = chain[meta[o_last + b]].astype(BF16)
         row_send[half + b] = chain[meta[o_last + half + rb + b]].astype(BF16)
-    row_ex = [
-        remote(row_send.at[pl.ds(0, half)], row_recv.at[pl.ds(half, half)], 6, left),
-        remote(row_send.at[pl.ds(half, half)], row_recv.at[pl.ds(0, half)], 7, right),
-    ]
-    for copy in row_ex:
-        copy.start()
+    row_ex = []
+    piece = half // 4
+    for k in range(4):
+        for j, (here, there, to) in enumerate(((0, half, left), (half, 0, right))):
+            src = row_send.at[pl.ds(here + k * piece, piece)]
+            dst = row_recv.at[pl.ds(there + k * piece, piece)]
+            row_ex.append(remote(src, dst, 8 + 2 * k + j, to))
+
+    def send_rows(k):
+        for copy in row_ex[2 * k : 2 * k + 2]:
+            copy.start()
+
+    send_rows(0)
     if len(stages) > 1:
         scatter_end(1, flying)
     if len(stages) > 2:
         flying = scatter_start(2)
+    send_rows(1)
 
     for copy in back_ex:
         copy.wait()
@@ -448,9 +465,15 @@
     mine = rows_at(base + digit * sub, sub)
     gathered[mine, :] = acc[mine, :].astype(BF16)
     for k in reversed(range(2, len(stages))):
-        for copy in gather_start(k):
+        copies = gather_start(k)
+        if k == 2:
+            send_rows(2)
+        for copy in copies:
             copy.wait()
+    if len(stages) < 3:
+        send_rows(2)
     flying = gather_start(1) if len(stages) > 1 else []
+    send_rows(3)
 
     put_out.wait()
     for copy in row_ex:
@@ -497,7 +520,7 @@
         out_shape=jax.ShapeDtypeStruct((2 * count + 4 * rb + win,), jnp.int32),
         in_specs=[smem] * 3,
         out_specs=smem,
-    )(block_cols, block_count, cluster_block)
+    )(block_cols.reshape(count), block_count, cluster_block)
 
     stages = stages_of(n)
     links = max(sum(radix - 1 for _, radix in stages), 1)
@@ -548,8 +571,8 @@
             pltpu.VMEM((max(rows, 16), width), BF16),
             pltpu.SemaphoreType.DMA((3,)),
             pltpu.SemaphoreType.DMA((2,)),
-            pltpu.SemaphoreType.DMA((8,)),
-            pltpu.SemaphoreType.DMA((8,)),
+            pltpu.SemaphoreType.DMA((16,)),
+            pltpu.SemaphoreType.DMA((16,)),
             pltpu.SemaphoreType.DMA((links,)),
             pltpu.SemaphoreType.DMA((links,)),
             pltpu.SemaphoreType.DMA((links,)),
@@ -580,8 +603,10 @@
         in_specs=[hbm] * 3,
         out_specs=[hbm, hbm] + [vmem] * 4,
         scratch_shapes=[
+            pltpu.VMEM(blocks, BF16),
+            pltpu.VMEM(blocks, BF16),
             pltpu.VMEM((height, width), BF16),
-            pltpu.SemaphoreType.DMA((2 * pieces + 1,)),
+            pltpu.SemaphoreType.DMA((2, 2 * pieces + 1)),
         ],
     )(*outs)
     return (outs[0].reshape(features.shape), outs[1].reshape(features.shape), *outs[2:])

time: 136 us -> 71.4 us (0.53)
  Pallas kernels: 134 us -> 69.2 us
    pallas_call x1, Pallas kernels: 65.7 us -> 3.54 us  [on_device(): pl.pallas_call(functools.partial(finish_kernel, pieces), out_shape=[jax.S...]
    pallas_call x1, Pallas kernels: 65.3 us -> 63.1 us  [on_device(): pl.pallas_call(functools.partial(kernel, (n, rb, slots, bs, cb)), out_sha...]
where the time goes in v2:
time: 71.4 us; the launch traced here: 71.2 us
  Pallas kernels  69.2 us (97%)
  local copies, waits for them, and re-layouts  1.36 us (2%)
    pallas_call x1, Pallas kernels, on_device(): pl.pallas_call(functools.partial(kernel, (n, rb, slots, bs, cb)), out_sha...  63.1 us
    pallas_call x1, Pallas kernels, on_device(): pl.pallas_call(functools.partial(finish_kernel, pieces), out_shape=[jax.S...  3.54 us
    pallas_call x1, Pallas kernels, on_device(): pl.pallas_call(functools.partial(order_kernel, (n, rb, slots, cb)), out_s...  2.48 us

profile of v2, /device:TPU:0, one launch (start us, length us, event | category | flops | bytes accessed | tf_op | source)
XLA Modules:
  0.0 71.2 jit_solution(9646352995907266146)
XLA Ops:
  0.6 0.8 %copy.18 = s32[16,8]{1,0:T(8,128)S(1)} copy(s32[16,8]{0,1:T(8,128)} %param.14) | data formatting | bytes 1024 | tf_op args[3]
  1.4 0.6 reshape.27.cols_in
  2.0 2.5 %shard_map.154.meta = s32[328]{0:T(512)} custom-call(s32[128]{0:T(128)} %reshape.27.cols_in, s32[16]{0:T(128)} %counts.1, s32[16]{0:T(128)} %clusters.1), custom_call_target="tpu_custom_call" | custom-call | tf_op jit(solution)/shard_map/pallas_call | solution.py:518
  4.5 63.1 %shard_map.155 = (bf16[16,128,256]{2,1,0:T(8,128)(2,1)}, bf16[16,128,256]{2,1,0:T(8,128)(2,1)}, bf16[1024,256]{1,0:T(8,128)(2,1)}) custom-call(s32[328]{0:T(512)} %shard_map.154.meta, s32[16,128]{1,0:T(8,128)} %slot.1, bf16[256,256]{1,0:T(8,128)(2,1)} %w_m.1, bf16[256,256]{1,0:T(8,128)(2,1)} %w_u.1, bf16[256,256]{1,0:T(8,128)(2,1)} %w_s.1, ...), custom_call_target="tpu_custom_call" | custom-call | tf_op jit(solution)/shard_map/pallas_call | solution.py:535
  67.6 3.5 %shard_map.156 = (bf16[16,128,256]{2,1,0:T(8,128)(2,1)}, bf16[16,128,256]{2,1,0:T(8,128)(2,1)}, f32[256,256]{1,0:T(8,128)}, f32[256,256]{1,0:T(8,128)}, f32[256,256]{1,0:T(8,128)}, /*index=5*/f32[256,256]{1,0:T(8,128)}) custom-call(bf16[16,128,256]{2,1,0:T(8,128)(2,1)} %get-tuple-element.15.a, bf16[16,128,256]{2,1,0:T(8,128)(2,1)} %get-tuple-element.16.b, ...), custom_call_target="tpu_custom_call" | custom-call | tf_op jit(solution)/shard_map/pallas_call | solution.py:596

commit v3 on v2

--- a/solution.py
+++ b/solution.py
@@ -314,8 +314,6 @@
         remote(back_send.at[pl.ds(0, cb)], back_recv.at[pl.ds(cb, cb)], 6, left),
         remote(back_send.at[pl.ds(cb, cb)], back_recv.at[pl.ds(0, cb)], 7, right),
     ]
-    for copy in back_ex:
-        copy.start()
 
     scale = 1.0 / math.sqrt(n * rb * bs)
     acc[...] = jnp.zeros_like(acc)
@@ -407,6 +405,8 @@
         return copies
 
     flying = scatter_start(0)
+    for copy in back_ex:
+        copy.start()
 
     def flow_body(r, carry):
         prod = mm(adj_t[r], back_m[r])
@@ -441,21 +441,6 @@
     if len(stages) > 2:
         flying = scatter_start(2)
     send_rows(1)
-
-    for copy in back_ex:
-        copy.wait()
-    for w in range(win):
-        rows = pl.ds(w * bs, bs)
-        summed = pool_chain[meta[o_lastc + w]] + back_recv[w].astype(F32)
-        g = (summed * c_slope[rows, :]).astype(BF16)
-        back_pooled[w] = mm_nt(g, w_c[...]).astype(BF16)
-
-    def spread_body(r, carry):
-        spread = mm(hot[r], back_pooled[meta[o_cidx + r]])
-        total[r] += 0.25 * spread + chain[meta[o_last + half + r]]
-        return carry
-
-    lax.fori_loop(0, rb, spread_body, 0, unroll=2)
 
     if len(stages) > 2:
         scatter_end(2, flying)
@@ -475,6 +460,24 @@
     flying = gather_start(1) if len(stages) > 1 else []
     send_rows(3)
 
+    for copy in back_ex:
+        copy.wait()
+    for w in range(win):
+        rows = pl.ds(w * bs, bs)
+        summed = pool_chain[meta[o_lastc + w]] + back_recv[w].astype(F32)
+        g = (summed * c_slope[rows, :]).astype(BF16)
+        back_pooled[w] = mm_nt(g, w_c[...]).astype(BF16)
+
+    def spread_body(r, carry):
+        spread = mm(hot[r], back_pooled[meta[o_cidx + r]])
+        total[r] += 0.25 * spread + chain[meta[o_last + half + r]]
+        return carry
+
+    lax.fori_loop(0, rb, spread_body, 0, unroll=2)
+
+    for copy in flying:
+        copy.wait()
+    flying = gather_start(0)
     put_out.wait()
     for copy in row_ex:
         copy.wait()
@@ -487,8 +490,6 @@
     put_grad = pltpu.make_async_copy(out_buf, feature_grad, out_sem.at[1])
     put_grad.start()
     for copy in flying:
-        copy.wait()
-    for copy in gather_start(0):
         copy.wait()
     put_grad.wait()
 

time: 71.4 us -> 70.4 us (0.986)
  Pallas kernels: 69.2 us -> 68.1 us
    pallas_call x1, Pallas kernels: 63.1 us -> 62.1 us  [on_device(): pl.pallas_call(functools.partial(kernel, (n, rb, slots, bs, cb)), out_sha...]
where the time goes in v3:
time: 70.4 us; the launch traced here: 70.1 us
  Pallas kernels  68.1 us (97%)
  local copies, waits for them, and re-layouts  1.36 us (2%)
    pallas_call x1, Pallas kernels, on_device(): pl.pallas_call(functools.partial(kernel, (n, rb, slots, bs, cb)), out_sha...  62.1 us
    pallas_call x1, Pallas kernels, on_device(): pl.pallas_call(functools.partial(finish_kernel, pieces), out_shape=[jax.S...  3.54 us
    pallas_call x1, Pallas kernels, on_device(): pl.pallas_call(functools.partial(order_kernel, (n, rb, slots, cb)), out_s...  2.48 us

profile of v3, /device:TPU:0, one launch (start us, length us, event | category | flops | bytes accessed | tf_op | source)
XLA Modules:
  0.0 70.1 jit_solution(7762781774098427446)
XLA Ops:
  0.6 0.8 %copy.18 = s32[16,8]{1,0:T(8,128)S(1)} copy(s32[16,8]{0,1:T(8,128)} %param.14) | data formatting | bytes 1024 | tf_op args[3]
  1.4 0.6 reshape.27.cols_in
  2.0 2.5 %shard_map.154.meta = s32[328]{0:T(512)} custom-call(s32[128]{0:T(128)} %reshape.27.cols_in, s32[16]{0:T(128)} %counts.1, s32[16]{0:T(128)} %clusters.1), custom_call_target="tpu_custom_call" | custom-call | tf_op jit(solution)/shard_map/pallas_call | solution.py:519
  4.5 62.1 %shard_map.155 = (bf16[16,128,256]{2,1,0:T(8,128)(2,1)}, bf16[16,128,256]{2,1,0:T(8,128)(2,1)}, bf16[1024,256]{1,0:T(8,128)(2,1)}) custom-call(s32[328]{0:T(512)} %shard_map.154.meta, s32[16,128]{1,0:T(8,128)} %slot.1, bf16[256,256]{1,0:T(8,128)(2,1)} %w_m.1, bf16[256,256]{1,0:T(8,128)(2,1)} %w_u.1, bf16[256,256]{1,0:T(8,128)(2,1)} %w_s.1, ...), custom_call_target="tpu_custom_call" | custom-call | tf_op jit(solution)/shard_map/pallas_call | solution.py:536
  66.6 3.5 %shard_map.156 = (bf16[16,128,256]{2,1,0:T(8,128)(2,1)}, bf16[16,128,256]{2,1,0:T(8,128)(2,1)}, f32[256,256]{1,0:T(8,128)}, f32[256,256]{1,0:T(8,128)}, f32[256,256]{1,0:T(8,128)}, /*index=5*/f32[256,256]{1,0:T(8,128)}) custom-call(bf16[16,128,256]{2,1,0:T(8,128)(2,1)} %get-tuple-element.15.a, bf16[16,128,256]{2,1,0:T(8,128)(2,1)} %get-tuple-element.16.b, ...), custom_call_target="tpu_custom_call" | custom-call | tf_op jit(solution)/shard_map/pallas_call | solution.py:597
